TPU v7x, 256 devices: a whole 4x4x8 slice. The times are simulated.
256 devices in a mesh: group: 8 (over z), store: 32 (over x, y, core).
Axes of the slice: x: 4, y: 4, z: 8, core: 2. Of those that a mesh axis runs over, the one named last changes fastest.
Arguments:
- features: bfloat16 [262144, 256], P(('group', 'store')), may hold values from -6 to 6
- past_hidden: bfloat16 [2, 262144, 256], P(None, ('group', 'store')), may hold values from 0 to 2
- past_grads: bfloat16 [2, 262144, 256], P(None, ('group', 'store')), may hold values from -6 to 6
- cotangent: bfloat16 [262144, 256], P(('group', 'store')), may hold values from -24 to 24
- weights: bfloat16 [3, 256, 256], replicated, may hold values from -0.375 to 0.375
- inner_tiles: bfloat16 [2048, 3, 128, 128], P(('group', 'store')), as said below
- inner_blocks: int32 [2048, 3], P(('group', 'store')), may hold values from 0 to 7, all different within a row
- outer_tiles: bfloat16 [2048, 3, 128, 128], P(('group', 'store')), as said below
- outer_blocks: int32 [2048, 3], P(('group', 'store')), may hold values from 0 to 7, all different within a row
- slot_rows: int32 [256, 1024], P(('group', 'store')), may hold values from 0 to 1023
- slot_counts: int32 [256, 32], P(('group', 'store')), may hold values from 1 to 32, as said below
Outputs:
- hidden_out: bfloat16 [3, 262144, 256], P(None, ('group', 'store'))
- grad_out: bfloat16 [2, 262144, 256], P(None, ('group', 'store'))
- weight_grad: float32 [3, 256, 256], replicated
Inputs may be any that keep to these rules, and one draw needn't show every extreme that they name: `slot_counts`: live halo slots of a device for one owner; every device has all 32 slots live for some owner, and some device for every owner. `slot_rows`: row within the owner's cluster; slots past the owner's count are padding. `inner_blocks`: distinct within a block row. `outer_blocks`: distinct within a block row. `inner_tiles`: nonnegative edge weights, most of them zero. `outer_tiles`: nonnegative edge weights, most of them zero.
All inputs are finite; a program needn't handle non-finite values.
Results may differ from a plain program's by a relative error of at most 0.0052.
Values may be sent and summed in bfloat16 or wider, within the bound.
A program may use at most 64 MiB of HBM per device.

v0:
```python
import math

import jax
import jax.numpy as jnp
from jax import lax
from jax.sharding import PartitionSpec as P

RESTART = 0.1


def beta_of(layer_idx):
    return math.log(0.5 / (layer_idx + 1) + 1.0)


def block_product(tile_set, block_ids, source):
    feat_dim = source.shape[-1]
    tile_len = tile_set.shape[-1]
    blocks = source.reshape(-1, tile_len, feat_dim)[block_ids]
    summed = jnp.einsum("bkij,bkjd->bid", tile_set, blocks, preferred_element_type=jnp.float32)
    return summed.reshape(-1, feat_dim)


def transposed_product(tile_set, block_ids, source):
    feat_dim = source.shape[-1]
    tile_len = tile_set.shape[-1]
    block_count = tile_set.shape[0]
    shaped = source.reshape(block_count, tile_len, feat_dim)
    pieces = jnp.einsum("bkij,bid->bkjd", tile_set, shaped, preferred_element_type=jnp.float32)
    choose = (
        block_ids[:, :, None] == jnp.arange(block_count, dtype=jnp.int32)[None, None, :]
    ).astype(jnp.float32)
    summed = jnp.einsum("bkc,bkjd->cjd", choose, pieces, precision=lax.Precision.HIGHEST)
    return summed.reshape(-1, feat_dim)


def per_device(
    features,
    past_hidden,
    past_grads,
    cotangent,
    weights,
    inner_tiles,
    inner_blocks,
    outer_tiles,
    outer_blocks,
    slot_rows,
    slot_counts,
):
    owners = lax.axis_size("store")
    node_total = features.shape[0] * lax.axis_size("group") * owners
    feat_dim = features.shape[1]
    halo_len = slot_rows.shape[1]
    per_owner = halo_len // owners
    layers = weights.shape[0]
    wanted = lax.all_to_all(
        slot_rows.reshape(owners, per_owner), "store", split_axis=0, concat_axis=0, tiled=True
    )
    live_mask = (jnp.arange(per_owner, dtype=jnp.int32)[None, :] < slot_counts[0][:, None])[
        :, :, None
    ]

    def pull_rows(source_table):
        arrived_rows = lax.all_to_all(
            source_table[wanted], "store", split_axis=0, concat_axis=0, tiled=True
        )
        arrived_rows = jnp.where(live_mask, arrived_rows, jnp.zeros((), arrived_rows.dtype))
        return arrived_rows.reshape(halo_len, feat_dim)

    first_f32 = features.astype(jnp.float32)
    hidden = features
    mixed_list = []
    pre_list = []
    hidden_list = []
    for layer_idx in range(layers):
        beta_now = beta_of(layer_idx)
        outside = pull_rows(features if layer_idx == 0 else past_hidden[layer_idx - 1])
        aggregate = block_product(inner_tiles, inner_blocks, hidden) + block_product(
            outer_tiles, outer_blocks, outside
        )
        mixed_rows = ((1.0 - RESTART) * aggregate + RESTART * first_f32).astype(jnp.bfloat16)
        projected = jnp.dot(mixed_rows, weights[layer_idx], preferred_element_type=jnp.float32)
        pre_act = (1.0 - beta_now) * mixed_rows.astype(jnp.float32) + beta_now * projected
        hidden = jax.nn.silu(pre_act).astype(jnp.bfloat16)
        mixed_list.append(mixed_rows)
        pre_list.append(pre_act)
        hidden_list.append(hidden)
    upstream = cotangent.astype(jnp.float32)
    w_terms = [None] * layers
    agg_grads = [None] * (layers - 1)
    for layer_idx in reversed(range(layers)):
        beta_now = beta_of(layer_idx)
        pre_act = pre_list[layer_idx]
        sigmoid_val = jax.nn.sigmoid(pre_act)
        pre_grad = (upstream * sigmoid_val * (1.0 + pre_act * (1.0 - sigmoid_val))).astype(
            jnp.bfloat16
        )
        w_term = beta_now * jnp.einsum(
            "nd,ne->de", mixed_list[layer_idx], pre_grad, preferred_element_type=jnp.float32
        )
        w_terms[layer_idx] = w_term
        if layer_idx >= 1:
            back_proj = jnp.einsum(
                "ne,de->nd", pre_grad, weights[layer_idx], preferred_element_type=jnp.float32
            )
            mix_grad = (1.0 - beta_now) * pre_grad.astype(jnp.float32) + beta_now * back_proj
            agg_grad = ((1.0 - RESTART) * mix_grad).astype(jnp.bfloat16)
            agg_grads[layer_idx - 1] = agg_grad
            outside = pull_rows(past_grads[layer_idx - 1])
            upstream = transposed_product(inner_tiles, inner_blocks, agg_grad) + block_product(
                outer_tiles, outer_blocks, outside
            )
    stacked = jnp.stack(w_terms)
    stacked = lax.psum(stacked, ("group", "store"))
    weight_grad = stacked * (1.0 / math.sqrt(node_total))
    return (jnp.stack(hidden_list), jnp.stack(agg_grads), weight_grad)


def solution(mesh):
    placed = (
        P(("group", "store"), None),
        P(None, ("group", "store"), None),
        P(None, ("group", "store"), None),
        P(("group", "store"), None),
        P(),
        P(("group", "store"), None, None, None),
        P(("group", "store"), None),
        P(("group", "store"), None, None, None),
        P(("group", "store"), None),
        P(("group", "store"), None),
        P(("group", "store"), None),
    )
    return jax.shard_map(
        per_device,
        mesh=mesh,
        in_specs=placed,
        out_specs=(P(None, ("group", "store"), None), P(None, ("group", "store"), None), P()),
        check_vma=False,
    )
```

profile of v0, /device:TPU:1, one launch (start us, length us, event | category | flops | bytes accessed | tf_op | source)
XLA Modules:
  0.0 442.6 jit_solution(2163626752311804927)
XLA Ops:
  9.7 8.6 %all-to-all-start = ((s32[32,1,32]{2,1,0:T(1,128)}), s32[32,1,32]{2,1,0:T(1,128)S(1)}, u32[]{:S(2)}, u32[]{:S(2)}) async-start(s32[32,1,32]{2,1,0:T(1,128)} %all_to_all.23), calls=%async_computation | async-start | bytes 32768 | tf_op jit(solution)/shard_map/all_to_all | solution.py:55
  19.6 5.6 %all-to-all-done = s32[32,1,32]{2,1,0:T(1,128)S(1)} async-done(((s32[32,1,32]{2,1,0:T(1,128)}), s32[32,1,32]{2,1,0:T(1,128)S(1)}, u32[]{:S(2)}, u32[]{:S(2)}) %all-to-all-start) | async-done | bytes 4128 | tf_op jit(solution)/shard_map/all_to_all | solution.py:55
  25.3 5.0 %gather_fusion.11 = bf16[1024,256]{1,0:T(8,128)(2,1)} fusion(bf16[1024,256]{1,0:T(8,128)(2,1)S(1)} %get-tuple-element.3, s32[1024]{0:T(1024)S(1)} %broadcast_clamp_fusion), kind=kCustom, calls=%fused_computation.11 | custom fusion | bytes 1052672 | tf_op jit(solution)/shard_map/gather | solution.py:64
  30.3 4.2 all-to-all-start.5
  35.7 5.0 %gather_fusion.4 = bf16[1024,256]{1,0:T(8,128)(2,1)} fusion(bf16[1024,256]{1,0:T(8,128)(2,1)S(1)} %get-tuple-element.7, s32[1024]{0:T(1024)S(1)} %broadcast_clamp_fusion), kind=kCustom, calls=%fused_computation.4 | custom fusion | bytes 1052672 | tf_op jit(solution)/shard_map/gather | solution.py:64
  40.7 5.5 %all-to-all-done.5 = bf16[32,32,256]{2,1,0:T(8,128)(2,1)S(1)} async-done(((bf16[32,32,256]{2,1,0:T(8,128)(2,1)}), bf16[32,32,256]{2,1,0:T(8,128)(2,1)S(1)}, u32[]{:S(2)}, u32[]{:S(2)}) %all-to-all-start.5) | async-done | bytes 524320 | tf_op jit(solution)/shard_map/all_to_all | solution.py:63
  46.2 3.7 all-to-all-start.2
  49.9 5.0 %gather_fusion.7 = bf16[1024,256]{1,0:T(8,128)(2,1)} fusion(bf16[1024,256]{1,0:T(8,128)(2,1)S(1)} %get-tuple-element.8, s32[1024]{0:T(1024)S(1)} %broadcast_clamp_fusion), kind=kCustom, calls=%fused_computation.7 | custom fusion | bytes 1052672 | tf_op jit(solution)/shard_map/gather | solution.py:64
  54.9 6.5 %all-to-all-done.2 = bf16[32,32,256]{2,1,0:T(8,128)(2,1)S(1)} async-done(((bf16[32,32,256]{2,1,0:T(8,128)(2,1)}), bf16[32,32,256]{2,1,0:T(8,128)(2,1)S(1)}, u32[]{:S(2)}, u32[]{:S(2)}) %all-to-all-start.2) | async-done | bytes 524320 | tf_op jit(solution)/shard_map/all_to_all | solution.py:63
  61.4 3.7 all-to-all-start.3
  65.1 5.0 %gather_fusion.9 = bf16[1024,256]{1,0:T(8,128)(2,1)} fusion(bf16[1024,256]{1,0:T(8,128)(2,1)S(1)} %get-tuple-element.4, s32[1024]{0:T(1024)S(1)} %broadcast_clamp_fusion), kind=kCustom, calls=%fused_computation.9 | custom fusion | bytes 1052672 | tf_op jit(solution)/shard_map/gather | solution.py:64
  70.1 6.6 %all-to-all-done.3 = bf16[32,32,256]{2,1,0:T(8,128)(2,1)S(1)} async-done(((bf16[32,32,256]{2,1,0:T(8,128)(2,1)}), bf16[32,32,256]{2,1,0:T(8,128)(2,1)S(1)}, u32[]{:S(2)}, u32[]{:S(2)}) %all-to-all-start.3) | async-done | bytes 524320 | tf_op jit(solution)/shard_map/all_to_all | solution.py:63
  76.7 3.7 all-to-all-start.4
  80.4 4.9 %gather_fusion.1 = bf16[1024,256]{1,0:T(8,128)(2,1)} fusion(bf16[1024,256]{1,0:T(8,128)(2,1)S(1)} %copy-done.1, s32[1024]{0:T(1024)S(1)} %broadcast_clamp_fusion), kind=kCustom, calls=%fused_computation.1 | custom fusion | bytes 1052672 | tf_op jit(solution)/shard_map/gather | solution.py:64
  85.4 6.6 %all-to-all-done.4 = bf16[32,32,256]{2,1,0:T(8,128)(2,1)S(1)} async-done(((bf16[32,32,256]{2,1,0:T(8,128)(2,1)}), bf16[32,32,256]{2,1,0:T(8,128)(2,1)S(1)}, u32[]{:S(2)}, u32[]{:S(2)}) %all-to-all-start.4) | async-done | bytes 524320 | tf_op jit(solution)/shard_map/all_to_all | solution.py:63
  91.9 4.4 all-to-all-start.1
  98.7 9.0 %all-to-all-done.1 = bf16[32,32,256]{2,1,0:T(8,128)(2,1)} async-done(((bf16[32,32,256]{2,1,0:T(8,128)(2,1)}), bf16[32,32,256]{2,1,0:T(8,128)(2,1)}, u32[]{:S(2)}, u32[]{:S(2)}) %all-to-all-start.1) | async-done | bytes 524320 | tf_op jit(solution)/shard_map/all_to_all | solution.py:63
  107.7 2.9 broadcast_select_fusion
  112.5 3.0 gather_fusion.5
  115.5 2.9 convolution_bitcast_fusion.2
  119.8 2.9 gather_fusion.2
  125.3 2.7 multiply_convert_fusion.3
  128.0 2.9 gather_fusion.3
  133.2 2.7 multiply_convert_fusion.2
  135.9 2.9 gather_fusion.6
  147.1 3.6 copy.29
  152.4 3.0 convolution_bitcast_fusion.9
  155.5 2.6 copy.30
  158.1 3.4 fusion.13
  167.7 3.6 copy.33
  175.6 3.1 fusion.14
  185.0 248.7 %all-reduce.2.cloned.1.call-done = f32[3,256,256]{2,1,0:T(8,128)} async-done(((f32[3,256,256]{2,1,0:T(8,128)}), f32[3,256,256]{2,1,0:T(8,128)}) %all-reduce.2.cloned.1.call-update) | async-done | bytes 786448 | tf_op jit(solution)/shard_map/psum | solution.py:113
  (105 shorter events, 44.5 us)
Async XLA Ops:
  7.2 117.5 %copy-start = (bf16[8,3,128,128]{3,2,1,0:T(8,128)(2,1)S(1)}, bf16[8,3,128,128]{3,2,1,0:T(8,128)(2,1)}, u32[]{:S(2)}) copy-start(bf16[8,3,128,128]{3,2,1,0:T(8,128)(2,1)} %param.16) | copy-start | bytes 2359300
  9.7 15.5 %all-to-all-start = ((s32[32,1,32]{2,1,0:T(1,128)}), s32[32,1,32]{2,1,0:T(1,128)S(1)}, u32[]{:S(2)}, u32[]{:S(2)}) async-start(s32[32,1,32]{2,1,0:T(1,128)} %all_to_all.23), calls=%async_computation | async-start | bytes 32768 | tf_op jit(solution)/shard_map/all_to_all | solution.py:55
  30.3 15.9 %all-to-all-start.5 = ((bf16[32,32,256]{2,1,0:T(8,128)(2,1)}), bf16[32,32,256]{2,1,0:T(8,128)(2,1)S(1)}, u32[]{:S(2)}, u32[]{:S(2)}) async-start(bf16[32,32,256]{2,1,0:T(8,128)(2,1)} %bitcast.64), calls=%async_computation.5 | async-start | bytes 1048576 | tf_op jit(solution)/shard_map/all_to_all | solution.py:63
  46.2 8.7 %copy-start.7 = (bf16[32,32,256]{2,1,0:T(8,128)(2,1)}, bf16[32,32,256]{2,1,0:T(8,128)(2,1)S(1)}, u32[]{:S(2)}) copy-start(bf16[32,32,256]{2,1,0:T(8,128)(2,1)S(1)} %all-to-all-done.5) | copy-start | bytes 1572868
  46.2 15.2 %all-to-all-start.2 = ((bf16[32,32,256]{2,1,0:T(8,128)(2,1)}), bf16[32,32,256]{2,1,0:T(8,128)(2,1)S(1)}, u32[]{:S(2)}, u32[]{:S(2)}) async-start(bf16[32,32,256]{2,1,0:T(8,128)(2,1)} %bitcast.20), calls=%async_computation.2 | async-start | bytes 1048576 | tf_op jit(solution)/shard_map/all_to_all | solution.py:63
  61.4 8.7 %copy-start.8 = (bf16[32,32,256]{2,1,0:T(8,128)(2,1)}, bf16[32,32,256]{2,1,0:T(8,128)(2,1)S(1)}, u32[]{:S(2)}) copy-start(bf16[32,32,256]{2,1,0:T(8,128)(2,1)S(1)} %all-to-all-done.2) | copy-start | bytes 1572868
  61.4 15.3 %all-to-all-start.3 = ((bf16[32,32,256]{2,1,0:T(8,128)(2,1)}), bf16[32,32,256]{2,1,0:T(8,128)(2,1)S(1)}, u32[]{:S(2)}, u32[]{:S(2)}) async-start(bf16[32,32,256]{2,1,0:T(8,128)(2,1)} %bitcast.34), calls=%async_computation.3 | async-start | bytes 1048576 | tf_op jit(solution)/shard_map/all_to_all | solution.py:63
  65.1 15.3 %copy-start.24 = (s32[8,3]{0,1:T(4,128)S(1)}, s32[8,3]{0,1:T(4,128)}, u32[]{:S(2)}) copy-start(s32[8,3]{0,1:T(4,128)} %param.19) | copy-start | bytes 292
  70.1 10.3 %copy-start.1 = (bf16[1024,256]{1,0:T(8,128)(2,1)S(1)}, bf16[1024,256]{1,0:T(8,128)(2,1)}, u32[]{:S(2)}) copy-start(bf16[1024,256]{1,0:T(8,128)(2,1)} %param.11) | copy-start | bytes 1572868
  76.7 8.7 %copy-start.9 = (bf16[32,32,256]{2,1,0:T(8,128)(2,1)}, bf16[32,32,256]{2,1,0:T(8,128)(2,1)S(1)}, u32[]{:S(2)}) copy-start(bf16[32,32,256]{2,1,0:T(8,128)(2,1)S(1)} %all-to-all-done.3) | copy-start | bytes 1572868
  76.7 15.3 %all-to-all-start.4 = ((bf16[32,32,256]{2,1,0:T(8,128)(2,1)}), bf16[32,32,256]{2,1,0:T(8,128)(2,1)S(1)}, u32[]{:S(2)}, u32[]{:S(2)}) async-start(bf16[32,32,256]{2,1,0:T(8,128)(2,1)} %bitcast.50), calls=%async_computation.4 | async-start | bytes 1048576 | tf_op jit(solution)/shard_map/all_to_all | solution.py:63
  80.4 16.0 %copy-start.23 = (s32[8,3]{0,1:T(4,128)S(1)}, s32[8,3]{0,1:T(4,128)}, u32[]{:S(2)}) copy-start(s32[8,3]{0,1:T(4,128)} %param.17) | copy-start | bytes 292
  91.9 6.7 %copy-start.10 = (bf16[32,32,256]{2,1,0:T(8,128)(2,1)}, bf16[32,32,256]{2,1,0:T(8,128)(2,1)S(1)}, u32[]{:S(2)}) copy-start(bf16[32,32,256]{2,1,0:T(8,128)(2,1)S(1)} %all-to-all-done.4) | copy-start | bytes 1572868
  91.9 15.8 %all-to-all-start.1 = ((bf16[32,32,256]{2,1,0:T(8,128)(2,1)}), bf16[32,32,256]{2,1,0:T(8,128)(2,1)}, u32[]{:S(2)}, u32[]{:S(2)}) async-start(bf16[32,32,256]{2,1,0:T(8,128)(2,1)} %bitcast.6), calls=%async_computation.1 | async-start | bytes 1048576 | tf_op jit(solution)/shard_map/all_to_all | solution.py:63
  96.3 337.3 %all-reduce.2.cloned.1.call-start = ((), (), s32[]{:S(2)}) async-start(), calls=%async_computation.6 | async-start | bytes 1572864 | tf_op jit(solution)/shard_map/psum | solution.py:113
  96.8 1.9 copy-start.25
  112.5 3.0 copy-start.2
  115.5 2.9 copy-start.6
  122.7 2.0 copy-start.5
  125.3 2.7 copy-start.17
  133.2 2.7 copy-start.20
  141.0 1.1 copy-start.27
  161.5 1.2 copy-start.16
  163.1 1.3 copy-start.21
  164.4 1.1 copy-start.13
  178.8 1.2 copy-start.15
  179.1 1.2 copy-start.18
  180.4 1.6 copy-start.12
  180.4 1.6 copy-start.14
  181.9 1.1 copy-start.3
  181.9 1.6 copy-start.4
  181.9 1.7 copy-start.19
  (3 other events, 2.8 us)
Sparse Core Ops, SparseCore 0:
  182.1 251.5 all-reduce.1
where the time goes:
time: 445 us; the launch traced here: 443 us
  waiting for transfers between devices  289 us (65%)
  local copies, waits for them, and re-layouts  63 us (14%)
  matrix products  37.5 us (8%)
  starting transfers between devices  28.3 us (6%)
  between operations  14.5 us (3%)
  other arithmetic  10.8 us (2%)
    psum x1, waiting for transfers between devices, per_device(): stacked = lax.psum(stacked, ('group', 'store'))  249 us
    all_to_all x5, waiting for transfers between devices, pull_rows(): lax.all_to_all(source_table[wanted], 'store', split_axis=0, concat_axis=0...  34.2 us
    gather x5, local copies, waits for them, and re-layouts, pull_rows(): source_table[wanted]  24.8 us
    all_to_all x5, starting transfers between devices, pull_rows(): lax.all_to_all(source_table[wanted], 'store', split_axis=0, concat_axis=0...  19.6 us
    gather x8, local copies, waits for them, and re-layouts, block_product(): blocks = source.reshape(-1, tile_len, feat_dim)[block_ids]  19 us
    dot_general x8, matrix products, block_product(): jnp.einsum('bkij,bkjd->bid', tile_set, blocks, preferred_element_type=jnp...  16.2 us
  transfers between devices with their start and end apart: 7, of which 7 were waited for; matrix products, arithmetic and copies ran while one was open for 6% of the time, Pallas kernels for 0%

commit v1 on v0

v1 whole, which is shorter than its diff:
```python
import functools
import math

import jax
import jax.numpy as jnp
from jax import lax
from jax.experimental import pallas as pl
from jax.experimental.pallas import tpu as pltpu
from jax.sharding import PartitionSpec as P

RESTART = 0.1
MESH = pl.DeviceIdType.MESH
BF = jnp.bfloat16
F32 = jnp.float32


def beta_of(layer_idx):
    return math.log(0.5 / (layer_idx + 1) + 1.0)


def dot(lhs, rhs):
    return jnp.dot(lhs, rhs, preferred_element_type=F32)


def dot_nt(lhs, rhs):
    return lax.dot_general(lhs, rhs, (((1,), (1,)), ((), ())), preferred_element_type=F32)


def step_kernel(
    groups, owners, node_total,
    feat_hbm, past_h_hbm, past_g_hbm, cot_hbm, w_hbm, itile_hbm, iblk_hbm, otile_hbm, oblk_hbm,
    rows_hbm, cnt_hbm,
    hid_hbm, gout_hbm, wg_hbm,
    table, cot, wts, itile, otile, iblk, oblk, cnt,
    idx, onehot, sendbuf, recv, a_in, a_out, a_int,
    hid, dsilu, mixt, agg, up, wterm, rs_recv, z_src, z_recv, wfull,
    lsem, idx_s, idx_r, tab_s, tab_r, rs_s, rs_r, z_s, z_r, ag_s, ag_r, osem,
):
    n_nodes, feat = table.shape[1], table.shape[2]
    layers = wts.shape[0]
    blocks, per_row, tile, _ = itile.shape
    cap = n_nodes // owners
    share = feat // owners
    g = lax.axis_index("group")
    s = lax.axis_index("store")

    def peer(i):
        return lax.rem(s + i, owners)

    def zpeer(i):
        return lax.rem(g + i, groups)

    loads = [
        pltpu.make_async_copy(feat_hbm, table.at[0], lsem.at[0]),
        pltpu.make_async_copy(cnt_hbm, cnt, lsem.at[1]),
        pltpu.make_async_copy(iblk_hbm, iblk, lsem.at[2]),
        pltpu.make_async_copy(oblk_hbm, oblk, lsem.at[3]),
        pltpu.make_async_copy(itile_hbm, itile, lsem.at[4]),
        pltpu.make_async_copy(otile_hbm, otile, lsem.at[5]),
        pltpu.make_async_copy(past_h_hbm, table.at[pl.ds(1, 2)], lsem.at[6]),
        pltpu.make_async_copy(past_g_hbm, table.at[pl.ds(3, 2)], lsem.at[7]),
        pltpu.make_async_copy(w_hbm, wts, lsem.at[8]),
        pltpu.make_async_copy(cot_hbm, cot, lsem.at[9]),
    ]
    for load in loads:
        load.start()

    barrier = pltpu.get_barrier_semaphore()

    def greet_store(i, carry):
        pl.semaphore_signal(barrier, inc=1, device_id=(g, peer(i)), device_id_type=MESH)
        return carry

    def greet_group(i, carry):
        pl.semaphore_signal(barrier, inc=1, device_id=(zpeer(i), s), device_id_type=MESH)
        return carry

    lax.fori_loop(1, owners, greet_store, 0)
    lax.fori_loop(1, groups, greet_group, 0)

    for load in loads[1:6]:
        load.wait()
    lane = lax.broadcasted_iota(jnp.int32, (1, tile), 1)
    per_chunk = tile // cap

    def build(b, carry):
        in_tiles = [itile[b, k] for k in range(per_row)]
        in_tiles_t = [t.T for t in in_tiles]
        out_tiles = [otile[b, k] for k in range(per_row)]
        for c in range(blocks):
            live_to = jnp.zeros((1, tile), jnp.int32)
            for q in range(per_chunk):
                live_to = jnp.where(lane // cap == q, cnt[0, c * per_chunk + q], live_to)
            live = (lane % cap < live_to).astype(F32)
            din = jnp.zeros((tile, tile), BF)
            dint = jnp.zeros((tile, tile), BF)
            dout = jnp.zeros((tile, tile), BF)
            for k in range(per_row):
                keep = (jnp.full((1, tile), iblk[b, k], jnp.int32) == c).astype(F32).astype(BF)
                din = din + in_tiles[k] * keep
                dint = dint + in_tiles_t[k] * keep
                keep = (live * (jnp.full((1, tile), oblk[b, k], jnp.int32) == c).astype(F32)).astype(BF)
                dout = dout + out_tiles[k] * keep
            rows = pl.ds(pl.multiple_of(b * tile, tile), tile)
            a_in[rows, pl.ds(c * tile, tile)] = din
            a_out[rows, pl.ds(c * tile, tile)] = dout
            a_int[pl.ds(c * tile, tile), rows] = dint
        return carry

    lax.fori_loop(0, blocks, build, 0)

    pl.semaphore_wait(barrier, owners - 1 + groups - 1)

    def idx_copy(i):
        o = peer(i)
        first = pl.multiple_of(o * cap // tile * tile, tile)
        return pltpu.make_async_remote_copy(
            src_ref=rows_hbm.at[:, pl.ds(first, tile)],
            dst_ref=idx.at[pl.ds(s, 1)],
            send_sem=idx_s, recv_sem=idx_r, device_id=(g, o), device_id_type=MESH,
        )

    def idx_start(i, carry):
        idx_copy(i).start()
        return carry

    lax.fori_loop(1, owners, idx_start, 0)
    own_first = pl.multiple_of(s * cap // tile * tile, tile)
    own_idx = pltpu.make_async_copy(rows_hbm.at[:, pl.ds(own_first, tile)], idx.at[pl.ds(s, 1)], lsem.at[10])
    own_idx.start()
    own_idx.wait()
    for load in (loads[0],) + tuple(loads[6:]):
        load.wait()
    for sem in (idx_r, idx_s):
        pltpu.make_async_copy(idx.at[pl.ds(0, owners - 1)], idx.at[pl.ds(0, owners - 1)], sem).wait()

    wanted_f = idx[...].astype(F32)
    per_step = 4

    def make_onehot(step, carry):
        rows_here = per_step * cap
        part = idx[pl.ds(pl.multiple_of(step * per_step, per_step), per_step)].astype(F32)
        spread = jnp.broadcast_to(part[:, None, :], (per_step, cap, tile)).reshape(rows_here, tile)
        place = lax.broadcasted_iota(jnp.int32, (rows_here, tile), 0) % cap + lax.rem(s, per_chunk) * cap
        at = lax.broadcasted_iota(jnp.int32, (rows_here, tile), 1)
        col = jnp.sum(jnp.where(place == at, spread, 0.0), axis=1, keepdims=True)
        node = lax.broadcasted_iota(jnp.int32, (rows_here, n_nodes), 1).astype(F32)
        onehot[pl.ds(pl.multiple_of(step * rows_here, rows_here), rows_here)] = jnp.where(
            node == col, 1.0, 0.0
        ).astype(BF)
        return carry

    lax.fori_loop(0, owners // per_step, make_onehot, 0)

    own_rows = pl.ds(pl.multiple_of(s * cap, cap), cap)
    chunk = 256
    n_chunk = n_nodes // chunk

    def rows_of(m):
        return pl.ds(pl.multiple_of(m * chunk, chunk), chunk)

    def pull(t):
        def gather(m, carry):
            sendbuf[t, rows_of(m)] = dot(onehot[rows_of(m)], table[t]).astype(BF)
            return carry

        lax.fori_loop(0, n_chunk, gather, 0)

        def send(i, carry):
            o = peer(i)
            pltpu.make_async_remote_copy(
                src_ref=sendbuf.at[t, pl.ds(pl.multiple_of(o * cap, cap), cap)],
                dst_ref=recv.at[t, own_rows],
                send_sem=tab_s.at[t], recv_sem=tab_r.at[t], device_id=(g, o), device_id_type=MESH,
            ).start()
            return carry

        lax.fori_loop(1, owners, send, 0)
        recv[t, own_rows] = sendbuf[t, own_rows]

    def wait_table(sem, t):
        part = recv.at[t, pl.ds(0, n_nodes - cap)]
        pltpu.make_async_copy(part, part, sem.at[t]).wait()

    order = (0, 1, 2, 4, 3)
    for t in order:
        pull(t)

    outs = []

    for l in range(layers):
        beta = beta_of(l)
        wait_table(tab_r, l)

        def forward(m, carry, l=l, beta=beta):
            r = rows_of(m)
            h_now = table[0] if l == 0 else hid[l - 1]
            total = dot(a_in[r], h_now) + dot(a_out[r], recv[l])
            mixed = ((1.0 - RESTART) * total + RESTART * table[0, r].astype(F32)).astype(BF)
            pre = (1.0 - beta) * mixed.astype(F32) + beta * dot(mixed, wts[l])
            q = jax.nn.sigmoid(pre)
            hid[l, r] = (pre * q).astype(BF)
            dsilu[l, r] = q * (1.0 + pre * (1.0 - q))
            mixt[l, :, r] = mixed.T
            return carry

        lax.fori_loop(0, n_chunk, forward, 0)
        outs.append(pltpu.make_async_copy(hid.at[l], hid_hbm.at[l], osem.at[l]))
        outs[-1].start()

    def rs_start(l):
        def go(i, carry):
            o = peer(i)
            pltpu.make_async_remote_copy(
                src_ref=wterm.at[l, pl.ds(pl.multiple_of(o * share, share), share)],
                dst_ref=rs_recv.at[l, pl.ds(pl.multiple_of(s * share, share), share)],
                send_sem=rs_s.at[l], recv_sem=rs_r.at[l], device_id=(g, o), device_id_type=MESH,
            ).start()
            return carry

        lax.fori_loop(1, owners, go, 0)
        own = pl.ds(pl.multiple_of(s * share, share), share)
        rs_recv[l, own] = wterm[l, own]

    def rs_end(l):
        part = rs_recv.at[l, pl.ds(0, feat - share)]
        pltpu.make_async_copy(part, part, rs_r.at[l]).wait()
        z_src[l] = jnp.sum(rs_recv[l].reshape(owners, share, feat), axis=0)

    def z_start(l):
        def go(i, carry):
            pltpu.make_async_remote_copy(
                src_ref=z_src.at[l], dst_ref=z_recv.at[l, pl.ds(pl.multiple_of(g * share, share), share)],
                send_sem=z_s.at[l], recv_sem=z_r.at[l], device_id=(zpeer(i), s), device_id_type=MESH,
            ).start()
            return carry

        lax.fori_loop(1, groups, go, 0)
        z_recv[l, pl.ds(pl.multiple_of(g * share, share), share)] = z_src[l]

    def z_end(l):
        part = z_recv.at[l, pl.ds(0, (groups - 1) * share)]
        pltpu.make_async_copy(part, part, z_r.at[l]).wait()
        total = jnp.sum(z_recv[l].reshape(groups, share, feat), axis=0)
        own = pl.ds(pl.multiple_of(s * share, share), share)
        wfull[l, own] = total * (beta_of(l) / math.sqrt(node_total))

    def ag_start(l):
        own = pl.ds(pl.multiple_of(s * share, share), share)

        def go(i, carry):
            pltpu.make_async_remote_copy(
                src_ref=wfull.at[l, own], dst_ref=wfull.at[l, own],
                send_sem=ag_s.at[l], recv_sem=ag_r.at[l], device_id=(g, peer(i)), device_id_type=MESH,
            ).start()
            return carry

        lax.fori_loop(1, owners, go, 0)

    def ag_end(l):
        part = wfull.at[l, pl.ds(0, feat - share)]
        pltpu.make_async_copy(part, part, ag_r.at[l]).wait()

    for l in reversed(range(layers)):
        beta = beta_of(l)
        if l == layers - 1:
            def first_up(m, carry):
                up[rows_of(m)] = cot[rows_of(m)].astype(F32)
                return carry

            lax.fori_loop(0, n_chunk, first_up, 0)
        else:
            src = l

            def inner_part(m, carry, src=src):
                up[rows_of(m)] = dot(a_int[rows_of(m)], agg[src])
                return carry

            lax.fori_loop(0, n_chunk, inner_part, 0)
            wait_table(tab_r, 3 + src)

            def outer_part(m, carry, src=src):
                up[rows_of(m)] += dot(a_out[rows_of(m)], recv[3 + src])
                return carry

            lax.fori_loop(0, n_chunk, outer_part, 0)

        wterm[l] = jnp.zeros((feat, feat), F32)

        def backward(m, carry, l=l, beta=beta):
            r = rows_of(m)
            pg = (up[r] * dsilu[l, r]).astype(BF)
            wterm[l] += dot(mixt[l, :, r], pg)
            if l >= 1:
                mix = (1.0 - beta) * pg.astype(F32) + beta * dot_nt(pg, wts[l])
                agg[l - 1, r] = ((1.0 - RESTART) * mix).astype(BF)
            return carry

        lax.fori_loop(0, n_chunk, backward, 0)
        rs_start(l)
        if l >= 1:
            outs.append(pltpu.make_async_copy(agg.at[l - 1], gout_hbm.at[l - 1], osem.at[layers + l - 1]))
            outs[-1].start()

    down = tuple(reversed(range(layers)))
    for l in down:
        rs_end(l)
        z_start(l)
    for l in down:
        z_end(l)
        ag_start(l)
    for l in down:
        ag_end(l)
    last = pltpu.make_async_copy(wfull, wg_hbm, osem.at[2 * layers - 1])
    last.start()

    for t in order:
        wait_table(tab_s, t)
    for l in down:
        for ref, sem, n in ((rs_recv, rs_s, feat - share), (z_recv, z_s, (groups - 1) * share), (wfull, ag_s, feat - share)):
            part = ref.at[l, pl.ds(0, n)]
            pltpu.make_async_copy(part, part, sem.at[l]).wait()
    for out in outs:
        out.wait()
    last.wait()


def per_device(features, past_hidden, past_grads, cotangent, weights, inner_tiles, inner_blocks,
               outer_tiles, outer_blocks, slot_rows, slot_counts):
    owners = lax.axis_size("store")
    groups = lax.axis_size("group")
    nodes, feat = features.shape
    layers = weights.shape[0]
    blocks, per_row, tile, _ = inner_tiles.shape
    node_total = nodes * owners * groups
    share = feat // owners
    anyspec = pl.BlockSpec(memory_space=pl.ANY)
    V = pltpu.VMEM
    S = pltpu.SemaphoreType.DMA
    return pl.pallas_call(
        functools.partial(step_kernel, groups, owners, node_total),
        out_shape=(
            jax.ShapeDtypeStruct((layers, nodes, feat), BF),
            jax.ShapeDtypeStruct((layers - 1, nodes, feat), BF),
            jax.ShapeDtypeStruct((layers, feat, feat), F32),
        ),
        in_specs=[anyspec] * 11,
        out_specs=(anyspec,) * 3,
        scratch_shapes=[
            V((5, nodes, feat), BF),
            V((nodes, feat), BF),
            V((layers, feat, feat), BF),
            V((blocks, per_row, tile, tile), BF),
            V((blocks, per_row, tile, tile), BF),
            pltpu.SMEM((blocks, per_row), jnp.int32),
            pltpu.SMEM((blocks, per_row), jnp.int32),
            pltpu.SMEM((1, owners), jnp.int32),
            V((owners, tile), jnp.int32),
            V((nodes, nodes), BF),
            V((5, nodes, feat), BF),
            V((5, nodes, feat), BF),
            V((nodes, nodes), BF),
            V((nodes, nodes), BF),
            V((nodes, nodes), BF),
            V((layers, nodes, feat), BF),
            V((layers, nodes, feat), F32),
            V((layers, feat, nodes), BF),
            V((layers - 1, nodes, feat), BF),
            V((nodes, feat), F32),
            V((layers, feat, feat), F32),
            V((layers, feat, feat), F32),
            V((layers, share, feat), F32),
            V((layers, groups * share, feat), F32),
            V((layers, feat, feat), F32),
            S((11,)), S, S, S((5,)), S((5,)),
            S((layers,)), S((layers,)), S((layers,)), S((layers,)), S((layers,)), S((layers,)),
            S((2 * layers,)),
        ],
        compiler_params=pltpu.CompilerParams(
            collective_id=0, has_side_effects=True, vmem_limit_bytes=56 << 20
        ),
        name="lmc_step",
    )(features, past_hidden, past_grads, cotangent, weights, inner_tiles, inner_blocks,
      outer_tiles, outer_blocks, slot_rows, slot_counts)


def solution(mesh):
    placed = (
        P(("group", "store"), None),
        P(None, ("group", "store"), None),
        P(None, ("group", "store"), None),
        P(("group", "store"), None),
        P(),
        P(("group", "store"), None, None, None),
        P(("group", "store"), None),
        P(("group", "store"), None, None, None),
        P(("group", "store"), None),
        P(("group", "store"), None),
        P(("group", "store"), None),
    )
    return jax.shard_map(
        per_device,
        mesh=mesh,
        in_specs=placed,
        out_specs=(P(None, ("group", "store"), None), P(None, ("group", "store"), None), P()),
        check_vma=False,
    )
```

time: 445 us -> 83.2 us (0.19)
  waiting for transfers between devices: 289 us -> 0 us
  Pallas kernels: 0 us -> 74.5 us
  local copies, waits for them, and re-layouts: 63 us -> 7.83 us
  matrix products: 37.5 us -> 0 us
  starting transfers between devices: 28.3 us -> 0 us
  between operations: 14.5 us -> 0.65 us
  other arithmetic: 10.8 us -> 0 us
    psum x1 -> x0, waiting for transfers between devices: 249 us -> none  [per_device(): stacked = lax.psum(stacked, ('group', 'store'))]
    pallas_call x0 -> x1, Pallas kernels: none -> 74.5 us  [per_device(): pl.pallas_call(functools.partial(step_kernel, groups, owners, node_total)...]
    gather x13 -> x0, local copies, waits for them, and re-layouts: 43.8 us -> none  [the longest x5 24.8 us: pull_rows(): source_table[wanted]]
    all_to_all x6 -> x0, waiting for transfers between devices: 39.8 us -> none  [the longest x5 34.2 us: pull_rows(): lax.all_to_all(source_table[wanted], 'store', split_axis=0, concat_axis=0...]
    dot_general x20 -> x0, matrix products: 37.5 us -> none  [the longest x8 16.2 us: block_product(): jnp.einsum('bkij,bkjd->bid', tile_set, blocks, preferred_element_type=jnp...]
    all_to_all x6 -> x0, starting transfers between devices: 28.2 us -> none  [the longest x5 19.6 us: pull_rows(): lax.all_to_all(source_table[wanted], 'store', split_axis=0, concat_axis=0...]
    dot_general x4 -> x0, local copies, waits for them, and re-layouts: 10.2 us -> none  [the longest x2 7.11 us: transposed_product(): jnp.einsum('bkij,bid->bkjd', tile_set, shaped, preferred_element_type=jnp...]
  transfers between devices with their start and end apart: 7 -> 0, of which waited for: 7 -> 0; matrix products, arithmetic and copies ran while one was open for 6% -> 0% of each run, Pallas kernels for 0% -> 0%
where the time goes in v1:
time: 83.2 us; the launch traced here: 83 us
  Pallas kernels  74.5 us (90%)
  local copies, waits for them, and re-layouts  7.83 us (9%)
    pallas_call x1, Pallas kernels, per_device(): pl.pallas_call(functools.partial(step_kernel, groups, owners, node_total)...  74.5 us
    unnamed x9, local copies, waits for them, and re-layouts  7.83 us

profile of v1, /device:TPU:1, one launch (start us, length us, event | category | flops | bytes accessed | tf_op | source)
XLA Modules:
  0.0 83.0 jit_solution(10621722015763536518)
XLA Ops:
  0.6 1.3 %copy.14.iblk_hbm = s32[8,3]{1,0:T(8,128)} copy(s32[8,3]{0,1:T(4,128)} %param.17) | data formatting | bytes 192 | tf_op args[6]
  2.0 1.3 %copy.15.oblk_hbm = s32[8,3]{1,0:T(8,128)} copy(s32[8,3]{0,1:T(4,128)} %param.19) | data formatting | bytes 192 | tf_op args[8]
  3.3 74.5 %lmc_step.1 = (bf16[3,1024,256]{2,1,0:T(8,128)(2,1)}, bf16[2,1024,256]{2,1,0:T(8,128)(2,1)}, f32[3,256,256]{2,1,0:T(8,128)}) custom-call(bf16[1024,256]{1,0:T(8,128)(2,1)} %feat_hbm.1, bf16[2,1024,256]{2,1,0:T(8,128)(2,1)} %past_h_hbm.1, bf16[2,1024,256]{2,1,0:T(8,128)(2,1)} %past_g_hbm.1, bf16[1024,256]{1,0:T(8,128)(2,1)} %cot_hbm.1, ...), custom_call_target="tpu_custom_call" | custom-call | tf_op jit(solution)/shard_map/lmc_step/pallas_call | solution.py:340
  77.8 0.0 copy-start
  77.8 2.7 %copy.19 = bf16[3,1024,256]{2,1,0:T(8,128)(2,1)} copy(bf16[3,1024,256]{2,1,0:T(8,128)(2,1)} %get-tuple-element.6) | data formatting | bytes 3145728
  80.6 0.0 copy-done
  80.6 0.0 copy-start.1
  80.6 1.0 %copy.20 = bf16[2,1024,256]{2,1,0:T(8,128)(2,1)} copy(bf16[2,1024,256]{2,1,0:T(8,128)(2,1)S(1)} %copy-done) | data formatting | bytes 2097152
  81.5 0.5 copy-done.1
  82.1 0.9 %copy.21 = f32[3,256,256]{2,1,0:T(8,128)} copy(f32[3,256,256]{2,1,0:T(8,128)S(1)} %copy-done.1) | data formatting | bytes 1572864
Async XLA Ops:
  77.8 2.8 %copy-start = (bf16[2,1024,256]{2,1,0:T(8,128)(2,1)S(1)}, bf16[2,1024,256]{2,1,0:T(8,128)(2,1)}, u32[]{:S(2)}) copy-start(bf16[2,1024,256]{2,1,0:T(8,128)(2,1)} %get-tuple-element.7) | copy-start | bytes 3145732
  80.6 1.5 %copy-start.1 = (f32[3,256,256]{2,1,0:T(8,128)S(1)}, f32[3,256,256]{2,1,0:T(8,128)}, u32[]{:S(2)}) copy-start(f32[3,256,256]{2,1,0:T(8,128)} %get-tuple-element.8) | copy-start | bytes 2359300

commit v2 on v1

v2 whole, which is shorter than its diff:
```python
import functools
import math

import jax
import jax.numpy as jnp
from jax import lax
from jax.experimental import pallas as pl
from jax.experimental.pallas import tpu as pltpu
from jax.sharding import PartitionSpec as P

RESTART = 0.1
MESH = pl.DeviceIdType.MESH
BF = jnp.bfloat16
F32 = jnp.float32


def beta_of(layer_idx):
    return math.log(0.5 / (layer_idx + 1) + 1.0)


def dot(lhs, rhs):
    return jnp.dot(lhs, rhs, preferred_element_type=F32)


def dot_nt(lhs, rhs):
    return lax.dot_general(lhs, rhs, (((1,), (1,)), ((), ())), preferred_element_type=F32)


def step_kernel(
    groups, owners, node_total,
    feat_hbm, past_h_hbm, past_g_hbm, cot_hbm, w_hbm, itile_hbm, iblk_hbm, otile_hbm, oblk_hbm,
    rows_hbm, cnt_hbm,
    hid, agg, wfull,
    table, cot, wts, itile, otile, iblk, oblk, cnt, rows, idx,
    onehot, sendbuf, recv, a_in, a_out, a_int, dsilu, mixt, up,
    wterm, core_recv, reduced, rs_recv, z_src, z_recv, wag,
    lsem, idx_s, idx_r, tab_s, tab_r, core_s, core_r, rs_s, rs_r, z_s, z_r, ag_s, ag_r,
):
    n_nodes, feat = table.shape[1], table.shape[2]
    layers = wts.shape[0]
    blocks, per_row, tile, _ = itile.shape
    cap = n_nodes // owners
    chips = owners // 2
    side = 4
    half = feat // 2
    share = feat // chips
    g = lax.axis_index("group")
    s = lax.axis_index("store")
    chip, core = s // 2, lax.rem(s, 2)
    cx, cy = chip // side, lax.rem(chip, side)

    def spread(j):
        return jnp.where(j == 0, 2, jnp.where(j == 1, 1, jnp.where(j == 2, 3, 0)))

    def chip_peer(j):
        return lax.rem(cx + spread(j // side), side) * side + lax.rem(cy + spread(lax.rem(j, side)), side)

    def peer(i):
        return chip_peer(i // 2) * 2 + lax.rem(core + 1 + lax.rem(i, 2), 2)

    def zpeer(i):
        mid = groups // 2
        return lax.rem(g + jnp.where(lax.rem(i, 2) == 0, mid + i // 2, mid - (i + 1) // 2), groups)

    ring = (2, 1, 3, 0)
    x_rows = [lax.rem(cx + a, side) for a in ring]
    steps = sorted(
        ((a, b, c) for a in range(side) for b in range(side) for c in range(2) if (a, b, c) != (0, 0, 0)),
        key=lambda p: -min(p[0], side - p[0]) - min(p[1], side - p[1]),
    )
    far = [
        (lax.rem(cx + a, side) * side + lax.rem(cy + b, side)) * 2 + lax.rem(core + c, 2) for a, b, c in steps
    ]
    far_chips = [
        lax.rem(cx + a, side) * side + lax.rem(cy + b, side) for a, b, c in steps if c == 0
    ]

    def each(count, act):
        def step(i, carry):
            act(i)
            return carry

        lax.fori_loop(0, count, step, 0)

    def block(index, size):
        return pl.ds(pl.multiple_of(index * size, size), size)

    def push(src, dst, send_sem, recv_sem, group, store):
        pltpu.make_async_remote_copy(
            src_ref=src, dst_ref=dst, send_sem=send_sem, recv_sem=recv_sem,
            device_id=(group, store), device_id_type=MESH,
        ).start()

    def drain(part, *sems):
        for sem in sems:
            pltpu.make_async_copy(part, part, sem).wait()

    loads = [
        pltpu.make_async_copy(src, dst, lsem.at[i])
        for i, (src, dst) in enumerate((
            (rows_hbm, rows),
            (cnt_hbm, cnt),
            (iblk_hbm, iblk),
            (oblk_hbm, oblk),
            (itile_hbm, itile),
            (otile_hbm, otile),
            (feat_hbm, table.at[0]),
            (past_h_hbm, table.at[pl.ds(1, 2)]),
            (past_g_hbm.at[1], table.at[3]),
            (past_g_hbm.at[0], table.at[4]),
            (w_hbm, wts),
            (cot_hbm, cot),
        ))
    ]
    for load in loads:
        load.start()

    barrier = pltpu.get_barrier_semaphore()
    each(owners - 1, lambda i: pl.semaphore_signal(
        barrier, inc=1, device_id=(g, peer(i)), device_id_type=MESH))
    each(groups - 1, lambda i: pl.semaphore_signal(
        barrier, inc=1, device_id=(zpeer(i), s), device_id_type=MESH))
    loads[0].wait()
    pl.semaphore_wait(barrier, owners - 1 + groups - 1)

    def wanted_lanes(o):
        return rows.at[:, pl.ds(pl.multiple_of(o * cap // tile * tile, tile), tile)]

    for o in far:
        push(wanted_lanes(o), idx.at[pl.ds(s, 1)], idx_s, idx_r, g, o)

    own_idx = pltpu.make_async_copy(wanted_lanes(s), idx.at[pl.ds(s, 1)], lsem.at[12])
    own_idx.start()

    for load in loads[1:6]:
        load.wait()
    lane = lax.broadcasted_iota(jnp.int32, (1, tile), 1)
    per_chunk = tile // cap

    def build(b):
        in_tiles = [itile[b, k] for k in range(per_row)]
        in_tiles_t = [t.T for t in in_tiles]
        out_tiles = [otile[b, k] for k in range(per_row)]
        for c in range(blocks):
            live_to = jnp.zeros((1, tile), jnp.int32)
            for q in range(per_chunk):
                live_to = jnp.where(lane // cap == q, cnt[0, c * per_chunk + q], live_to)
            live = (lane % cap < live_to).astype(F32)
            din = jnp.zeros((tile, tile), BF)
            dint = jnp.zeros((tile, tile), BF)
            dout = jnp.zeros((tile, tile), BF)
            for k in range(per_row):
                keep = (jnp.full((1, tile), iblk[k, b], jnp.int32) == c).astype(F32).astype(BF)
                din = din + in_tiles[k] * keep
                dint = dint + in_tiles_t[k] * keep
                keep = (live * (jnp.full((1, tile), oblk[k, b], jnp.int32) == c).astype(F32)).astype(BF)
                dout = dout + out_tiles[k] * keep
            here = block(b, tile)
            a_in[here, pl.ds(c * tile, tile)] = din
            a_out[here, pl.ds(c * tile, tile)] = dout
            a_int[pl.ds(c * tile, tile), here] = dint

    each(blocks, build)
    own_idx.wait()
    for load in loads[6:]:
        load.wait()
    drain(idx.at[pl.ds(0, owners - 1)], idx_r, idx_s)

    chunk = n_nodes // side
    n_chunk = side
    per_quarter = owners // side

    def make_onehot(quarter):
        part = idx[block(quarter, per_quarter)].astype(F32)
        wide = jnp.broadcast_to(part[:, None, :], (per_quarter, cap, tile)).reshape(chunk, tile)
        place = lax.broadcasted_iota(jnp.int32, (chunk, tile), 0) % cap + lax.rem(s, per_chunk) * cap
        at = lax.broadcasted_iota(jnp.int32, (chunk, tile), 1)
        col = jnp.sum(jnp.where(place == at, wide, 0.0), axis=1, keepdims=True)
        node = lax.broadcasted_iota(jnp.int32, (chunk, n_nodes), 1).astype(F32)
        hot = jnp.where(node == col, 1.0, 0.0).astype(BF)
        onehot[block(quarter, chunk)] = hot
        return hot

    def send_rows(t, o):
        push(sendbuf.at[t, block(o, cap)], recv.at[t, block(s, cap)], tab_s.at[t], tab_r.at[t], g, o)

    def gather(t, quarter, hot):
        sendbuf[t, block(quarter, chunk)] = dot(hot, table[t]).astype(BF)

    for j in range(side):
        gather(0, x_rows[j], make_onehot(x_rows[j]))
    for o in far:
        send_rows(0, o)
    recv[0, block(s, cap)] = sendbuf[0, block(s, cap)]

    def pull_next(t):
        t = t + 1
        for quarter in range(side):
            gather(t, quarter, onehot[block(quarter, chunk)])
        for o in far:
            send_rows(t, o)
        recv[t, block(s, cap)] = sendbuf[t, block(s, cap)]

    each(table.shape[0] - 1, pull_next)

    def arrived(t):
        drain(recv.at[t, pl.ds(0, n_nodes - cap)], tab_r.at[t])

    for l in range(layers):
        beta = beta_of(l)
        arrived(l)

        def forward(m, l=l, beta=beta):
            r = block(m, chunk)
            h_now = table[0] if l == 0 else hid[l - 1]
            total = dot(a_in[r], h_now) + dot(a_out[r], recv[l])
            mixed = ((1.0 - RESTART) * total + RESTART * table[0, r].astype(F32)).astype(BF)
            pre = (1.0 - beta) * mixed.astype(F32) + beta * dot(mixed, wts[l])
            q = jax.nn.sigmoid(pre)
            hid[l, r] = (pre * q).astype(BF)
            dsilu[l, r] = q * (1.0 + pre * (1.0 - q))
            mixt[l, :, r] = mixed.T

        each(n_chunk, forward)

    def core_start(l):
        push(wterm.at[l, 1 - core], core_recv.at[l], core_s.at[l], core_r.at[l], g, chip * 2 + 1 - core)

    def core_end(l):
        drain(core_recv.at[l], core_r.at[l])
        reduced[l] = wterm[l, core] + core_recv[l]

    def rs_start(l):
        def go(k):
            push(reduced.at[l, block(k, share)], rs_recv.at[l, block(chip, share)],
                 rs_s.at[l], rs_r.at[l], g, k * 2 + core)

        if l == 0:
            for k in far_chips:
                go(k)
        else:
            each(chips - 1, lambda j: go(chip_peer(j)))
        rs_recv[l, block(chip, share)] = reduced[l, block(chip, share)]

    def rs_end(l):
        drain(rs_recv.at[l, pl.ds(0, feat - share)], rs_r.at[l])
        z_src[l] = jnp.sum(rs_recv[l].reshape(chips, share, half), axis=0)

    def z_start(l):
        each(groups - 1, lambda i: push(
            z_src.at[l], z_recv.at[l, block(g, share)], z_s.at[l], z_r.at[l], zpeer(i), s))
        z_recv[l, block(g, share)] = z_src[l]

    def z_end(l):
        drain(z_recv.at[l, pl.ds(0, (groups - 1) * share)], z_r.at[l])
        total = jnp.sum(z_recv[l].reshape(groups, share, half), axis=0)
        wag[l, block(core * chips + chip, share)] = (
            total * (beta_of(l) / math.sqrt(node_total))).astype(BF)

    def ag_start(l):
        own = block(core * chips + chip, share)

        def go(o):
            push(wag.at[l, own], wag.at[l, own], ag_s.at[l], ag_r.at[l], g, o)

        if l == 0:
            for o in far:
                go(o)
        else:
            each(owners - 1, lambda i: go(peer(i)))

    def ag_end(l):
        drain(wag.at[l, pl.ds(0, 2 * feat - share)], ag_r.at[l])
        for c in range(2):
            wfull[l, :, c * half:(c + 1) * half] = wag[l, c * feat:(c + 1) * feat].astype(F32)

    for l in reversed(range(layers)):
        beta = beta_of(l)
        if l < layers - 1:
            def inner_part(m, l=l):
                up[block(m, chunk)] = dot(a_int[block(m, chunk)], agg[l])

            each(n_chunk, inner_part)
            core_end(l + 1)
            rs_start(l + 1)
            t = 2 * layers - 2 - l
            arrived(t)
        wsum = [None, None]
        for m in range(n_chunk):
            r = pl.ds(m * chunk, chunk)
            if l == layers - 1:
                above = cot[r].astype(F32)
            else:
                above = up[r] + dot(a_out[r], recv[t])
            pg = (above * dsilu[l, r]).astype(BF)
            part = dot(mixt[l, :, r], pg)
            for c in range(2):
                cols = part[:, c * half:(c + 1) * half]
                wsum[c] = cols if m == 0 else wsum[c] + cols
            if l >= 1:
                mix = (1.0 - beta) * pg.astype(F32) + beta * dot_nt(pg, wts[l])
                agg[l - 1, r] = ((1.0 - RESTART) * mix).astype(BF)
        for c in range(2):
            wterm[l, c] = wsum[c]
        core_start(l)

    down = tuple(reversed(range(layers)))
    core_end(0)
    rs_start(0)
    for l in down:
        rs_end(l)
        z_start(l)
    for l in down:
        z_end(l)
        ag_start(l)
    for l in down:
        ag_end(l)

    for t in range(table.shape[0]):
        drain(recv.at[t, pl.ds(0, n_nodes - cap)], tab_s.at[t])
    for l in down:
        drain(core_recv.at[l], core_s.at[l])
        drain(rs_recv.at[l, pl.ds(0, feat - share)], rs_s.at[l])
        drain(z_recv.at[l, pl.ds(0, (groups - 1) * share)], z_s.at[l])
        drain(wag.at[l, pl.ds(0, 2 * feat - share)], ag_s.at[l])


def store_kernel(hid, agg, wfull, hid_hbm, agg_hbm, wg_hbm, sem):
    copies = [
        pltpu.make_async_copy(src, dst, sem.at[i])
        for i, (src, dst) in enumerate(((hid, hid_hbm), (agg, agg_hbm), (wfull, wg_hbm)))
    ]
    for copy in copies:
        copy.start()
    for copy in copies:
        copy.wait()


def per_device(features, past_hidden, past_grads, cotangent, weights, inner_tiles, inner_blocks,
               outer_tiles, outer_blocks, slot_rows, slot_counts):
    owners = lax.axis_size("store")
    groups = lax.axis_size("group")
    nodes, feat = features.shape
    layers = weights.shape[0]
    blocks, per_row, tile, _ = inner_tiles.shape
    node_total = nodes * owners * groups
    share = feat // (owners // 2)
    anyspec = pl.BlockSpec(memory_space=pltpu.HBM)
    V = pltpu.VMEM
    S = pltpu.SemaphoreType.DMA
    res = pl.pallas_call(
        functools.partial(step_kernel, groups, owners, node_total),
        out_shape=(
            V((layers, nodes, feat), BF),
            V((layers - 1, nodes, feat), BF),
            V((layers, feat, feat), F32),
        ),
        in_specs=[anyspec] * 11,
        out_specs=(pl.BlockSpec(memory_space=V),) * 3,
        scratch_shapes=[
            V((5, nodes, feat), BF),
            V((nodes, feat), BF),
            V((layers, feat, feat), BF),
            V((blocks, per_row, tile, tile), BF),
            V((blocks, per_row, tile, tile), BF),
            pltpu.SMEM((per_row, blocks), jnp.int32),
            pltpu.SMEM((per_row, blocks), jnp.int32),
            pltpu.SMEM((1, owners), jnp.int32),
            V((1, nodes), jnp.int32),
            V((owners, tile), jnp.int32),
            V((nodes, nodes), BF),
            V((5, nodes, feat), BF),
            V((5, nodes, feat), BF),
            V((nodes, nodes), BF),
            V((nodes, nodes), BF),
            V((nodes, nodes), BF),
            V((layers, nodes, feat), F32),
            V((layers, feat, nodes), BF),
            V((nodes, feat), F32),
            V((layers, 2, feat, feat // 2), F32),
            V((layers, feat, feat // 2), F32),
            V((layers, feat, feat // 2), F32),
            V((layers, feat, feat // 2), F32),
            V((layers, share, feat // 2), F32),
            V((layers, groups * share, feat // 2), F32),
            V((layers, 2 * feat, feat // 2), BF),
            S((13,)), S, S, S((5,)), S((5,)),
            S((layers,)), S((layers,)), S((layers,)), S((layers,)),
            S((layers,)), S((layers,)), S((layers,)), S((layers,)),
        ],
        compiler_params=pltpu.CompilerParams(
            collective_id=0, has_side_effects=True, vmem_limit_bytes=60 << 20
        ),
        name="lmc_step",
    )(features, past_hidden, past_grads, cotangent, weights, inner_tiles, inner_blocks.T,
      outer_tiles, outer_blocks.T, slot_rows, slot_counts)
    return pl.pallas_call(
        store_kernel,
        out_shape=tuple(jax.ShapeDtypeStruct(r.shape, r.dtype) for r in res),
        in_specs=[pl.BlockSpec(memory_space=V)] * 3,
        out_specs=(anyspec,) * 3,
        scratch_shapes=[S((3,))],
        compiler_params=pltpu.CompilerParams(vmem_limit_bytes=1 << 20),
        name="store_results",
    )(*[pltpu.with_memory_space_constraint(r, V) for r in res])


def solution(mesh):
    placed = (
        P(("group", "store"), None),
        P(None, ("group", "store"), None),
        P(None, ("group", "store"), None),
        P(("group", "store"), None),
        P(),
        P(("group", "store"), None, None, None),
        P(("group", "store"), None),
        P(("group", "store"), None, None, None),
        P(("group", "store"), None),
        P(("group", "store"), None),
        P(("group", "store"), None),
    )
    return jax.shard_map(
        per_device,
        mesh=mesh,
        in_specs=placed,
        out_specs=(P(None, ("group", "store"), None), P(None, ("group", "store"), None), P()),
        check_vma=False,
    )
```

time: 83.2 us -> 69.5 us (0.84)
  local copies, waits for them, and re-layouts: 7.83 us -> 0 us
  Pallas kernels: 74.5 us -> 68.7 us
    unnamed x9 -> x0, local copies, waits for them, and re-layouts: 7.83 us -> none
    pallas_call x1, Pallas kernels: 74.5 us -> 67 us  [per_device(): pl.pallas_call(functools.partial(step_kernel, groups, owners, node_total)...]
    pallas_call x0 -> x1, Pallas kernels: none -> 1.77 us  [per_device(): pl.pallas_call(store_kernel, out_shape=tuple((jax.ShapeDtypeStruct(r.shap...]
where the time goes in v2:
time: 69.5 us; the launch traced here: 69.4 us
  Pallas kernels  68.7 us (99%)
    pallas_call x1, Pallas kernels, per_device(): pl.pallas_call(functools.partial(step_kernel, groups, owners, node_total)...  67 us
    pallas_call x1, Pallas kernels, per_device(): pl.pallas_call(store_kernel, out_shape=tuple((jax.ShapeDtypeStruct(r.shap...  1.77 us

profile of v2, /device:TPU:1, one launch (start us, length us, event | category | flops | bytes accessed | tf_op | source)
XLA Modules:
  0.0 69.4 jit_solution(5668241467645751066)
XLA Ops:
  0.6 67.0 %lmc_step.1 = (bf16[3,1024,256]{2,1,0:T(8,128)(2,1)S(1)}, bf16[2,1024,256]{2,1,0:T(8,128)(2,1)S(1)}, f32[3,256,256]{2,1,0:T(8,128)S(1)}) custom-call(bf16[1024,256]{1,0:T(8,128)(2,1)} %feat_hbm.1, bf16[2,1024,256]{2,1,0:T(8,128)(2,1)} %past_h_hbm.1, bf16[2,1024,256]{2,1,0:T(8,128)(2,1)} %past_g_hbm.1, bf16[1024,256]{1,0:T(8,128)(2,1)} %cot_hbm.1, ...), custom_call_target="tpu_custom_call" | custom-call | tf_op jit(solution)/shard_map/lmc_step/pallas_call | solution.py:351
  67.6 1.8 %store_results.1 = (bf16[3,1024,256]{2,1,0:T(8,128)(2,1)}, bf16[2,1024,256]{2,1,0:T(8,128)(2,1)}, f32[3,256,256]{2,1,0:T(8,128)}) custom-call(bf16[3,1024,256]{2,1,0:T(8,128)(2,1)S(1)} %get-tuple-element.6.hid, bf16[2,1024,256]{2,1,0:T(8,128)(2,1)S(1)} %get-tuple-element.7.agg, f32[3,256,256]{2,1,0:T(8,128)S(1)} %get-tuple-element.8.wfull), custom_call_target="tpu_custom_call" | custom-call | tf_op jit(solution)/shard_map/store_results/pallas_call | solution.py:397

commit v3 on v2

--- a/solution.py
+++ b/solution.py
@@ -32,7 +32,7 @@
     rows_hbm, cnt_hbm,
     hid, agg, wfull,
     table, cot, wts, itile, otile, iblk, oblk, cnt, rows, idx,
-    onehot, sendbuf, recv, a_in, a_out, a_int, dsilu, mixt, up,
+    onehot, sendbuf, recv, a_in, a_out, a_int, dsilu, mixt, mixed_last, pgs, up,
     wterm, core_recv, reduced, rs_recv, z_src, z_recv, wag,
     lsem, idx_s, idx_r, tab_s, tab_r, core_s, core_r, rs_s, rs_r, z_s, z_r, ag_s, ag_r,
 ):
@@ -66,7 +66,7 @@
     x_rows = [lax.rem(cx + a, side) for a in ring]
     steps = sorted(
         ((a, b, c) for a in range(side) for b in range(side) for c in range(2) if (a, b, c) != (0, 0, 0)),
-        key=lambda p: -min(p[0], side - p[0]) - min(p[1], side - p[1]),
+        key=lambda p: (-min(p[0], side - p[0]) - min(p[1], side - p[1]), p[2], (p[0] + 2 * p[1]) % 4, p),
     )
     far = [
         (lax.rem(cx + a, side) * side + lax.rem(cy + b, side)) * 2 + lax.rem(core + c, 2) for a, b, c in steps
@@ -112,14 +112,15 @@
             (cot_hbm, cot),
         ))
     ]
-    for load in loads:
-        load.start()
+    loads[0].start()
 
     barrier = pltpu.get_barrier_semaphore()
-    each(owners - 1, lambda i: pl.semaphore_signal(
-        barrier, inc=1, device_id=(g, peer(i)), device_id_type=MESH))
     each(groups - 1, lambda i: pl.semaphore_signal(
         barrier, inc=1, device_id=(zpeer(i), s), device_id_type=MESH))
+    for o in far:
+        pl.semaphore_signal(barrier, inc=1, device_id=(g, o), device_id_type=MESH)
+    for load in loads[1:]:
+        load.start()
     loads[0].wait()
     pl.semaphore_wait(barrier, owners - 1 + groups - 1)
 
@@ -170,38 +171,32 @@
     n_chunk = side
     per_quarter = owners // side
 
+    ranked = far + [s]
+
     def make_onehot(quarter):
-        part = idx[block(quarter, per_quarter)].astype(F32)
+        asked = [idx[pl.ds(o, 1)] for o in ranked[quarter * per_quarter:(quarter + 1) * per_quarter]]
+        part = jnp.concatenate(asked, axis=0).astype(F32)
         wide = jnp.broadcast_to(part[:, None, :], (per_quarter, cap, tile)).reshape(chunk, tile)
         place = lax.broadcasted_iota(jnp.int32, (chunk, tile), 0) % cap + lax.rem(s, per_chunk) * cap
         at = lax.broadcasted_iota(jnp.int32, (chunk, tile), 1)
         col = jnp.sum(jnp.where(place == at, wide, 0.0), axis=1, keepdims=True)
         node = lax.broadcasted_iota(jnp.int32, (chunk, n_nodes), 1).astype(F32)
         hot = jnp.where(node == col, 1.0, 0.0).astype(BF)
-        onehot[block(quarter, chunk)] = hot
+        onehot[pl.ds(quarter * chunk, chunk)] = hot
         return hot
 
-    def send_rows(t, o):
-        push(sendbuf.at[t, block(o, cap)], recv.at[t, block(s, cap)], tab_s.at[t], tab_r.at[t], g, o)
-
-    def gather(t, quarter, hot):
-        sendbuf[t, block(quarter, chunk)] = dot(hot, table[t]).astype(BF)
-
-    for j in range(side):
-        gather(0, x_rows[j], make_onehot(x_rows[j]))
-    for o in far:
-        send_rows(0, o)
-    recv[0, block(s, cap)] = sendbuf[0, block(s, cap)]
-
-    def pull_next(t):
-        t = t + 1
+    def pull(t, hot_of):
         for quarter in range(side):
-            gather(t, quarter, onehot[block(quarter, chunk)])
-        for o in far:
-            send_rows(t, o)
-        recv[t, block(s, cap)] = sendbuf[t, block(s, cap)]
-
-    each(table.shape[0] - 1, pull_next)
+            first = quarter * per_quarter
+            sendbuf[t, pl.ds(quarter * chunk, chunk)] = dot(hot_of(quarter), table[t]).astype(BF)
+            for i in range(first, first + per_quarter):
+                if i < owners - 1:
+                    push(sendbuf.at[t, pl.ds(i * cap, cap)], recv.at[t, block(s, cap)],
+                         tab_s.at[t], tab_r.at[t], g, ranked[i])
+        recv[t, block(s, cap)] = sendbuf[t, pl.ds((owners - 1) * cap, cap)]
+
+    pull(0, make_onehot)
+    each(table.shape[0] - 1, lambda t: pull(t + 1, lambda quarter: onehot[pl.ds(quarter * chunk, chunk)]))
 
     def arrived(t):
         drain(recv.at[t, pl.ds(0, n_nodes - cap)], tab_r.at[t])
@@ -211,17 +206,22 @@
         arrived(l)
 
         def forward(m, l=l, beta=beta):
-            r = block(m, chunk)
+            r = pl.ds(m * chunk, chunk)
             h_now = table[0] if l == 0 else hid[l - 1]
             total = dot(a_in[r], h_now) + dot(a_out[r], recv[l])
             mixed = ((1.0 - RESTART) * total + RESTART * table[0, r].astype(F32)).astype(BF)
             pre = (1.0 - beta) * mixed.astype(F32) + beta * dot(mixed, wts[l])
             q = jax.nn.sigmoid(pre)
-            hid[l, r] = (pre * q).astype(BF)
-            dsilu[l, r] = q * (1.0 + pre * (1.0 - q))
-            mixt[l, :, r] = mixed.T
-
-        each(n_chunk, forward)
+            act = pre * q
+            hid[l, r] = act.astype(BF)
+            dsilu[l, r] = q + act * (1.0 - q)
+            if l < layers - 1:
+                mixt[l, :, r] = mixed.T
+            else:
+                mixed_last[r] = mixed
+
+        for m in range(n_chunk):
+            forward(m)
 
     def core_start(l):
         push(wterm.at[l, 1 - core], core_recv.at[l], core_s.at[l], core_r.at[l], g, chip * 2 + 1 - core)
@@ -274,18 +274,33 @@
         for c in range(2):
             wfull[l, :, c * half:(c + 1) * half] = wag[l, c * feat:(c + 1) * feat].astype(F32)
 
+    def weight_term(l, pgs):
+        wsum = [None, None]
+        for m, pg in enumerate(pgs):
+            r = pl.ds(m * chunk, chunk)
+            part = dot(mixt[l, :, r], pg)
+            for c in range(2):
+                cols = part[:, c * half:(c + 1) * half]
+                wsum[c] = cols if m == 0 else wsum[c] + cols
+        for c in range(2):
+            wterm[l, c] = wsum[c]
+        core_start(l)
+
     for l in reversed(range(layers)):
         beta = beta_of(l)
         if l < layers - 1:
-            def inner_part(m, l=l):
-                up[block(m, chunk)] = dot(a_int[block(m, chunk)], agg[l])
-
-            each(n_chunk, inner_part)
+            for m in range(n_chunk):
+                r = pl.ds(m * chunk, chunk)
+                up[r] = dot(a_int[r], agg[l])
+            if l == layers - 2:
+                for m in range(n_chunk):
+                    r = pl.ds(m * chunk, chunk)
+                    mixt[l + 1, :, r] = mixed_last[r].T
+            weight_term(l + 1, [pgs[pl.ds(m * chunk, chunk)] for m in range(n_chunk)])
             core_end(l + 1)
             rs_start(l + 1)
             t = 2 * layers - 2 - l
             arrived(t)
-        wsum = [None, None]
         for m in range(n_chunk):
             r = pl.ds(m * chunk, chunk)
             if l == layers - 1:
@@ -293,16 +308,11 @@
             else:
                 above = up[r] + dot(a_out[r], recv[t])
             pg = (above * dsilu[l, r]).astype(BF)
-            part = dot(mixt[l, :, r], pg)
-            for c in range(2):
-                cols = part[:, c * half:(c + 1) * half]
-                wsum[c] = cols if m == 0 else wsum[c] + cols
+            pgs[r] = pg
             if l >= 1:
                 mix = (1.0 - beta) * pg.astype(F32) + beta * dot_nt(pg, wts[l])
                 agg[l - 1, r] = ((1.0 - RESTART) * mix).astype(BF)
-        for c in range(2):
-            wterm[l, c] = wsum[c]
-        core_start(l)
+    weight_term(0, [pgs[pl.ds(m * chunk, chunk)] for m in range(n_chunk)])
 
     down = tuple(reversed(range(layers)))
     core_end(0)
@@ -376,6 +386,8 @@
             V((nodes, nodes), BF),
             V((layers, nodes, feat), F32),
             V((layers, feat, nodes), BF),
+            V((nodes, feat), BF),
+            V((nodes, feat), BF),
             V((nodes, feat), F32),
             V((layers, 2, feat, feat // 2), F32),
             V((layers, feat, feat // 2), F32),

time: 69.5 us -> 68.9 us (level)
  no operation moved by 1% of the time
where the time goes in v3:
time: 68.9 us; the launch traced here: 68.8 us
  Pallas kernels  68.1 us (99%)
    pallas_call x1, Pallas kernels, per_device(): pl.pallas_call(functools.partial(step_kernel, groups, owners, node_total)...  66.4 us
    pallas_call x1, Pallas kernels, per_device(): pl.pallas_call(store_kernel, out_shape=tuple((jax.ShapeDtypeStruct(r.shap...  1.77 us

profile of v3, /device:TPU:1, one launch (start us, length us, event | category | flops | bytes accessed | tf_op | source)
XLA Modules:
  0.0 68.8 jit_solution(7301372291151812241)
XLA Ops:
  0.6 66.4 %lmc_step.1 = (bf16[3,1024,256]{2,1,0:T(8,128)(2,1)S(1)}, bf16[2,1024,256]{2,1,0:T(8,128)(2,1)S(1)}, f32[3,256,256]{2,1,0:T(8,128)S(1)}) custom-call(bf16[1024,256]{1,0:T(8,128)(2,1)} %feat_hbm.1, bf16[2,1024,256]{2,1,0:T(8,128)(2,1)} %past_h_hbm.1, bf16[2,1024,256]{2,1,0:T(8,128)(2,1)} %past_g_hbm.1, bf16[1024,256]{1,0:T(8,128)(2,1)} %cot_hbm.1, ...), custom_call_target="tpu_custom_call" | custom-call | tf_op jit(solution)/shard_map/lmc_step/pallas_call | solution.py:361
  67.0 1.8 %store_results.1 = (bf16[3,1024,256]{2,1,0:T(8,128)(2,1)}, bf16[2,1024,256]{2,1,0:T(8,128)(2,1)}, f32[3,256,256]{2,1,0:T(8,128)}) custom-call(bf16[3,1024,256]{2,1,0:T(8,128)(2,1)S(1)} %get-tuple-element.6.hid, bf16[2,1024,256]{2,1,0:T(8,128)(2,1)S(1)} %get-tuple-element.7.agg, f32[3,256,256]{2,1,0:T(8,128)S(1)} %get-tuple-element.8.wfull), custom_call_target="tpu_custom_call" | custom-call | tf_op jit(solution)/shard_map/store_results/pallas_call | solution.py:409

commit v4 on v3

--- a/solution.py
+++ b/solution.py
@@ -235,7 +235,7 @@
             push(reduced.at[l, block(k, share)], rs_recv.at[l, block(chip, share)],
                  rs_s.at[l], rs_r.at[l], g, k * 2 + core)
 
-        if l == 0:
+        if l <= 1:
             for k in far_chips:
                 go(k)
         else:
@@ -297,8 +297,9 @@
                     r = pl.ds(m * chunk, chunk)
                     mixt[l + 1, :, r] = mixed_last[r].T
             weight_term(l + 1, [pgs[pl.ds(m * chunk, chunk)] for m in range(n_chunk)])
-            core_end(l + 1)
-            rs_start(l + 1)
+            if l >= 1:
+                core_end(l + 1)
+                rs_start(l + 1)
             t = 2 * layers - 2 - l
             arrived(t)
         for m in range(n_chunk):
@@ -315,6 +316,8 @@
     weight_term(0, [pgs[pl.ds(m * chunk, chunk)] for m in range(n_chunk)])
 
     down = tuple(reversed(range(layers)))
+    core_end(1)
+    rs_start(1)
     core_end(0)
     rs_start(0)
     for l in down:
@@ -323,16 +326,15 @@
     for l in down:
         z_end(l)
         ag_start(l)
-    for l in down:
-        ag_end(l)
-
     for t in range(table.shape[0]):
         drain(recv.at[t, pl.ds(0, n_nodes - cap)], tab_s.at[t])
     for l in down:
         drain(core_recv.at[l], core_s.at[l])
         drain(rs_recv.at[l, pl.ds(0, feat - share)], rs_s.at[l])
         drain(z_recv.at[l, pl.ds(0, (groups - 1) * share)], z_s.at[l])
+    for l in down:
         drain(wag.at[l, pl.ds(0, 2 * feat - share)], ag_s.at[l])
+        ag_end(l)
 
 
 def store_kernel(hid, agg, wfull, hid_hbm, agg_hbm, wg_hbm, sem):

time: 68.9 us -> 68 us (0.987)
  Pallas kernels: 68.1 us -> 67.2 us
    pallas_call x1, Pallas kernels: 66.4 us -> 65.4 us  [per_device(): pl.pallas_call(functools.partial(step_kernel, groups, owners, node_total)...]
where the time goes in v4:
time: 68 us; the launch traced here: 67.9 us
  Pallas kernels  67.2 us (99%)
    pallas_call x1, Pallas kernels, per_device(): pl.pallas_call(functools.partial(step_kernel, groups, owners, node_total)...  65.4 us
    pallas_call x1, Pallas kernels, per_device(): pl.pallas_call(store_kernel, out_shape=tuple((jax.ShapeDtypeStruct(r.shap...  1.77 us

profile of v4, /device:TPU:1, one launch (start us, length us, event | category | flops | bytes accessed | tf_op | source)
XLA Modules:
  0.0 67.9 jit_solution(10844324160266339453)
XLA Ops:
  0.6 65.4 %lmc_step.1 = (bf16[3,1024,256]{2,1,0:T(8,128)(2,1)S(1)}, bf16[2,1024,256]{2,1,0:T(8,128)(2,1)S(1)}, f32[3,256,256]{2,1,0:T(8,128)S(1)}) custom-call(bf16[1024,256]{1,0:T(8,128)(2,1)} %feat_hbm.1, bf16[2,1024,256]{2,1,0:T(8,128)(2,1)} %past_h_hbm.1, bf16[2,1024,256]{2,1,0:T(8,128)(2,1)} %past_g_hbm.1, bf16[1024,256]{1,0:T(8,128)(2,1)} %cot_hbm.1, ...), custom_call_target="tpu_custom_call" | custom-call | tf_op jit(solution)/shard_map/lmc_step/pallas_call | solution.py:363
  66.1 1.8 %store_results.1 = (bf16[3,1024,256]{2,1,0:T(8,128)(2,1)}, bf16[2,1024,256]{2,1,0:T(8,128)(2,1)}, f32[3,256,256]{2,1,0:T(8,128)}) custom-call(bf16[3,1024,256]{2,1,0:T(8,128)(2,1)S(1)} %get-tuple-element.6.hid, bf16[2,1024,256]{2,1,0:T(8,128)(2,1)S(1)} %get-tuple-element.7.agg, f32[3,256,256]{2,1,0:T(8,128)S(1)} %get-tuple-element.8.wfull), custom_call_target="tpu_custom_call" | custom-call | tf_op jit(solution)/shard_map/store_results/pallas_call | solution.py:411
